TPU v7x, 32 devices: a whole 2x2x4 slice. The times are simulated.
32 devices in a mesh: req: 8 (over z, x), head: 4 (over y, core).
Axes of the slice: x: 2, y: 2, z: 4, core: 2. Of those that a mesh axis runs over, the one named last changes fastest.
Arguments:
- tokens: bfloat16 [8192, 1536], P('req', 'head'), may hold values from -6 to 6
- new_counts: int32 [8, 4], P('req'), may hold values from 1 to 512, 1024 in all within a row
- kv_cache: bfloat16 [32, 8, 7680, 128], P('req', 'head'), may hold values from -300 to 300
- norm_attn: float32 [1536], replicated, may hold values from 0.1 to 1.9
- query_weight: bfloat16 [1536, 8, 192], P(None, 'head'), may hold values from -0.15625 to 0.15625
- key_value_weight: bfloat16 [1536, 8, 128], P(None, 'head'), may hold values from -0.4375 to 0.4375
- output_weight: bfloat16 [8, 192, 1536], P('head'), may hold values from -0.15625 to 0.15625
- norm_moe: float32 [1536], replicated, may hold values from 0.1 to 1.9
- routes: int32 [8192, 8], P(('req', 'head')), may hold values from 0 to 31, all different within a row; in each aligned block of 256 rows (0 to 255, 256 to 511, ...) at most 128 rows name the same one
- route_gain: float32 [8192, 8], P(('req', 'head')), may hold values from 0.03 to 0.3
- w_gate_up: bfloat16 [32, 1536, 1024], P('req'), may hold values from -0.15625 to 0.15625
- w_down: bfloat16 [32, 512, 1536], P('req'), may hold values from -0.25 to 0.25
Outputs:
- mixed: bfloat16 [8192, 1536], P(('req', 'head'))
Inputs may be any that keep to these rules, and one draw needn't show every extreme that they name: `new_counts`: the 4 counts of one index of req sum to 1024, and one of them is exactly 512. `routes`: the 8 experts of a row differ. In each aligned block of 256 rows (the rows of one device) no expert is named more than 128 times, a bound that some block reaches.
All inputs are finite; a program needn't handle non-finite values.
Results may differ from a plain program's by a relative error of at most 0.019.
Values may be sent and summed in bfloat16 or wider, within the bound.
A program may use at most 192 MiB of HBM per device.

v0:
```python
import math

import jax
import jax.numpy as jnp
from jax import lax
from jax.sharding import PartitionSpec as P

EXPERTS = 32
TOPK = 8
RATIO = 15


floor_score = -1e30


def norm_rows(value_rows, gain_row):
    mean_square = jnp.mean(value_rows * value_rows, axis=-1, keepdims=True)
    return value_rows * lax.rsqrt(mean_square + 1e-05) * gain_row


def rope_tables(position, head_size):
    half_size = head_size // 2
    inverse = jnp.exp(
        jnp.arange(half_size, dtype=jnp.float32) * (-2.0 * math.log(10000.0) / head_size)
    )
    angles = position.astype(jnp.float32)[:, None] * inverse[None, :]
    angles = jnp.concatenate([angles, angles], axis=1)
    return (jnp.cos(angles), jnp.sin(angles))


def rotate(vectors, cos_part, sin_part):
    half_size = vectors.shape[-1] // 2
    turned = jnp.concatenate([-vectors[..., half_size:], vectors[..., :half_size]], axis=-1)
    return vectors * cos_part + turned * sin_part


def request_layout(counts, token_count, cache_ratio):
    end_rows = jnp.cumsum(counts)
    starts = end_rows - counts
    row_ids = jnp.arange(token_count, dtype=jnp.int32)
    segment = jnp.sum((row_ids[:, None] >= end_rows[None, :]).astype(jnp.int32), axis=1)
    member = (segment[:, None] == jnp.arange(counts.shape[0], dtype=jnp.int32)[None, :]).astype(
        jnp.int32
    )
    row_begin = jnp.sum(member * starts[None, :], axis=1)
    own_count = jnp.sum(member * counts[None, :], axis=1)
    position = cache_ratio * own_count + row_ids - row_begin
    return (starts, position)


def project(normed, query_weight, key_value_weight, position):
    token_count, model_width = normed.shape
    kv_heads = key_value_weight.shape[1]
    head_size = key_value_weight.shape[2] // 2
    group_size = query_weight.shape[2] // head_size
    query = jnp.dot(
        normed, query_weight.reshape(model_width, -1), preferred_element_type=jnp.float32
    )
    query = query.reshape(token_count, kv_heads, group_size, head_size)
    keyval = jnp.dot(
        normed, key_value_weight.reshape(model_width, -1), preferred_element_type=jnp.float32
    )
    keyval = keyval.reshape(token_count, kv_heads, 2 * head_size)
    cos_part, sin_part = rope_tables(position, head_size)
    query = rotate(query, cos_part[:, None, None, :], sin_part[:, None, None, :]).astype(
        jnp.bfloat16
    )
    new_key = rotate(keyval[..., :head_size], cos_part[:, None, :], sin_part[:, None, :]).astype(
        jnp.bfloat16
    )
    new_value = keyval[..., head_size:].astype(jnp.bfloat16)
    return (query, new_key, new_value)


def absorb(carried, scores, usable, value_rows, pattern):
    highest, denominator, numerator = carried
    scores = jnp.where(usable, scores, floor_score)
    new_top = jnp.maximum(highest, jnp.max(scores, axis=-1))
    rescale = jnp.exp(highest - new_top)
    weights = jnp.where(usable, jnp.exp(scores - new_top[..., None]), 0.0)
    denominator = denominator * rescale + jnp.sum(weights, axis=-1)
    numerator = numerator * rescale[..., None] + jnp.einsum(
        pattern, weights.astype(jnp.bfloat16), value_rows, preferred_element_type=jnp.float32
    )
    return (new_top, denominator, numerator)


def local(
    tokens,
    new_counts,
    kv_cache,
    norm_attn,
    query_weight,
    key_value_weight,
    output_weight,
    norm_moe,
    routes,
    route_gain,
    w_gate_up,
    w_down,
):
    whole = lax.all_gather(tokens, "head", axis=1, tiled=True)
    token_count, model_width = whole.shape
    normed = norm_rows(whole.astype(jnp.float32), norm_attn).astype(jnp.bfloat16)
    counts = new_counts[0]
    starts, position = request_layout(counts, token_count, RATIO)
    query, new_key, new_value = project(normed, query_weight, key_value_weight, position)
    kv_heads, group_size, head_size = (query.shape[1], query.shape[2], query.shape[3])
    window = token_count // 2
    key_block = 3 * window
    score_scale = 1.0 / math.sqrt(head_size)
    stat_shape = (kv_heads, group_size, window)

    def one_request(which, result):
        row_begin = starts[which]
        count_here = counts[which]
        cached = RATIO * count_here
        win_start = jnp.minimum(row_begin, token_count - window)
        row_ids = win_start + jnp.arange(window, dtype=jnp.int32)
        inside = (row_ids >= row_begin) & (row_ids < row_begin + count_here)
        q_win = lax.dynamic_slice_in_dim(query, win_start, window, 0)
        k_win = lax.dynamic_slice_in_dim(new_key, win_start, window, 0)
        v_win = lax.dynamic_slice_in_dim(new_value, win_start, window, 0)
        p_win = lax.dynamic_slice_in_dim(position, win_start, window, 0)
        past = lax.dynamic_index_in_dim(kv_cache, which, 0, keepdims=False)

        def key_step(block_index, carried):
            key_piece = lax.dynamic_slice_in_dim(past, block_index * key_block, key_block, 1)
            slot_ids = block_index * key_block + jnp.arange(key_block, dtype=jnp.int32)
            usable = (slot_ids < cached)[None, None, None, :]
            scores = (
                jnp.einsum(
                    "qhgd,hkd->hgqk",
                    q_win,
                    key_piece[..., :head_size],
                    preferred_element_type=jnp.float32,
                )
                * score_scale
            )
            return absorb(carried, scores, usable, key_piece[..., head_size:], "hgqk,hkd->hgqd")

        start_state = (
            jnp.full(stat_shape, floor_score, jnp.float32),
            jnp.zeros(stat_shape, jnp.float32),
            jnp.zeros(stat_shape + (head_size,), jnp.float32),
        )
        block_count = (cached + key_block - 1) // key_block
        carried = lax.fori_loop(0, block_count, key_step, start_state)
        new_ok = (inside[None, :] & (p_win[None, :] <= p_win[:, None]))[None, None, :, :]
        scores = (
            jnp.einsum("qhgd,khd->hgqk", q_win, k_win, preferred_element_type=jnp.float32)
            * score_scale
        )
        highest, denominator, numerator = absorb(carried, scores, new_ok, v_win, "hgqk,khd->hgqd")
        attended = jnp.transpose(numerator / denominator[..., None], (2, 0, 1, 3))
        current = lax.dynamic_slice_in_dim(result, win_start, window, 0)
        update = jnp.where(inside[:, None, None, None], attended, current)
        return lax.dynamic_update_slice_in_dim(result, update, win_start, 0)

    initial = jnp.zeros(query.shape, jnp.float32)
    result = lax.fori_loop(0, counts.shape[0], one_request, initial)
    attn_out = result.astype(jnp.bfloat16).reshape(token_count, -1)
    partial_value = jnp.dot(
        attn_out, output_weight.reshape(-1, model_width), preferred_element_type=jnp.float32
    )
    per_block = routes.shape[0]
    row_start = lax.axis_index("head") * per_block
    summed = lax.psum(partial_value.astype(jnp.bfloat16), "head").astype(jnp.float32)
    attn_rows = lax.dynamic_slice_in_dim(summed, row_start, per_block, 0)
    base_rows = lax.dynamic_slice_in_dim(whole, row_start, per_block, 0)
    resid = base_rows.astype(jnp.float32) + attn_rows
    moe_in = norm_rows(resid, norm_moe).astype(jnp.bfloat16)
    capacity = per_block // 2
    flat_routes = routes.reshape(-1)
    expert_ids = jnp.arange(EXPERTS, dtype=jnp.int32)
    onehot = (flat_routes[:, None] == expert_ids[None, :]).astype(jnp.int32)
    before = jnp.cumsum(onehot, axis=0) - onehot
    rank_in = jnp.sum(before * onehot, axis=1)
    slot_ids = flat_routes * capacity + rank_in
    owners = jnp.arange(per_block * TOPK, dtype=jnp.int32) // TOPK
    table = jnp.full((EXPERTS * capacity,), per_block, jnp.int32).at[slot_ids].set(owners)
    padded = jnp.concatenate([moe_in, jnp.zeros((1, model_width), jnp.bfloat16)], axis=0)
    req_count = lax.axis_size("req")
    per_req = w_down.shape[0]
    ff_width = w_down.shape[1]
    outgoing = padded[table].reshape(req_count, per_req, capacity, model_width)
    gate_up = jnp.einsum(
        "sncd,ndf->sncf",
        lax.all_to_all(outgoing, "req", split_axis=0, concat_axis=0, tiled=True),
        w_gate_up,
        preferred_element_type=jnp.float32,
    )
    hidden = (jax.nn.silu(gate_up[..., :ff_width]) * gate_up[..., ff_width:]).astype(jnp.bfloat16)
    produced = jnp.einsum(
        "sncf,nfd->sncd", hidden, w_down, preferred_element_type=jnp.float32
    ).astype(jnp.bfloat16)
    arrived = lax.all_to_all(produced, "req", split_axis=0, concat_axis=0, tiled=True)
    gathered = arrived.reshape(EXPERTS * capacity, model_width)[slot_ids].astype(jnp.float32)
    gathered = gathered.reshape(per_block, TOPK, model_width)
    moe_sum = jnp.sum(gathered * route_gain[..., None], axis=1)
    return (resid + moe_sum).astype(jnp.bfloat16)


def solution(mesh):
    in_specs = (
        P("req", "head"),
        P("req", None),
        P("req", "head", None, None),
        P(),
        P(None, "head", None),
        P(None, "head", None),
        P("head", None, None),
        P(),
        P(("req", "head"), None),
        P(("req", "head"), None),
        P("req", None, None),
        P("req", None, None),
    )
    out_specs = P(("req", "head"), None)
    return jax.shard_map(local, mesh=mesh, in_specs=in_specs, out_specs=out_specs, check_vma=False)
```

profile of v0, /device:TPU:0, one launch (start us, length us, event | category | flops | bytes accessed | tf_op | source)
XLA Modules:
  0.0 1091.9 jit_solution(8461358803930505704)
XLA Ops:
  15.1 25.0 %all-gather.2.cloned.1.call-done = bf16[1024,1536]{1,0:T(8,128)(2,1)} async-done(((bf16[1024,384]{1,0:T(8,128)(2,1)}), bf16[1024,1536]{1,0:T(8,128)(2,1)}) %all-gather.2.cloned.1.call-update) | async-done | bytes 3145744 | tf_op jit(solution)/shard_map/all_gather | solution.py:102
  50.6 284.0 %while.88 = (s32[]{:T(128)}, bf16[1024,2,3,64]{0,3,2,1:T(8,128)(2,1)}, s32[4]{0:T(128)S(1)}, s32[4]{0:T(128)S(1)}, bf16[4,2,7680,128]{3,2,1,0:T(8,128)(2,1)}, /*...) while((s32[]{:T(128)}, ...), condition=%wide.region_12.13_spmd, body=%wide.region_5.12_spmd.sunk | while | flops 1694123008 | bytes 104254264 | solution.py:161
  60.1 6.3 copy.75
  66.6 31.8 %while.89 = (s32[]{:T(128)}, f32[2,3,512]{2,1,0:T(4,128)S(1)}, f32[2,3,512]{2,1,0:T(4,128)S(1)}, f32[2,3,512,64]{2,3,1,0:T(8,128)S(1)}, s32[]{:T(128)}, /*index=...) while((s32[]{:T(128)}, f32[2,3,512]{2,1,0:T(4,128)S(1)}, ...), condition=%wide.region_9.9_spmd, body=%wide.region_6.8_spmd.sunk | while | flops 1269703680 | bytes 59589324 | solution.py:148
  71.1 5.9 fusion.113
  119.3 6.3 copy.75
  125.7 79.6 %while.89 = (s32[]{:T(128)}, f32[2,3,512]{2,1,0:T(4,128)S(1)}, f32[2,3,512]{2,1,0:T(4,128)S(1)}, f32[2,3,512,64]{2,3,1,0:T(8,128)S(1)}, s32[]{:T(128)}, /*index=...) while((s32[]{:T(128)}, f32[2,3,512]{2,1,0:T(4,128)S(1)}, ...), condition=%wide.region_9.9_spmd, body=%wide.region_6.8_spmd.sunk | while | flops 1269703680 | bytes 59589324 | solution.py:148
  146.1 5.9 fusion.113
  211.5 5.9 dynamic_update_slice.15
  226.8 6.3 copy.75
  233.2 31.8 %while.89 = (s32[]{:T(128)}, f32[2,3,512]{2,1,0:T(4,128)S(1)}, f32[2,3,512]{2,1,0:T(4,128)S(1)}, f32[2,3,512,64]{2,3,1,0:T(8,128)S(1)}, s32[]{:T(128)}, /*index=...) while((s32[]{:T(128)}, f32[2,3,512]{2,1,0:T(4,128)S(1)}, ...), condition=%wide.region_9.9_spmd, body=%wide.region_6.8_spmd.sunk | while | flops 1269703680 | bytes 59589324 | solution.py:148
  285.3 6.3 copy.75
  291.7 31.8 %while.89 = (s32[]{:T(128)}, f32[2,3,512]{2,1,0:T(4,128)S(1)}, f32[2,3,512]{2,1,0:T(4,128)S(1)}, f32[2,3,512,64]{2,3,1,0:T(8,128)S(1)}, s32[]{:T(128)}, /*index=...) while((s32[]{:T(128)}, f32[2,3,512]{2,1,0:T(4,128)S(1)}, ...), condition=%wide.region_9.9_spmd, body=%wide.region_6.8_spmd.sunk | while | flops 1269703680 | bytes 59589324 | solution.py:148
  339.7 9.1 reduce-window.11
  349.7 8.1 scatter_custom_fusion
  357.8 67.3 %all-reduce.3.cloned.1.call-done = bf16[1024,1536]{1,0:T(8,128)(2,1)} async-done(((bf16[1024,1536]{1,0:T(8,128)(2,1)}), bf16[1024,1536]{1,0:T(8,128)(2,1)}) %all-reduce.3.cloned.1.call-update) | async-done | bytes 3145744 | tf_op jit(solution)/shard_map/psum | solution.py:168
  428.5 19.2 %gather_fusion = bf16[4096,1536]{1,0:T(8,128)(2,1)} fusion(bf16[257,1536]{1,0:T(8,128)(2,1)S(1)} %concatenate.31, s32[4096]{0:T(1024)S(1)} %fusion.81), kind=kCustom, calls=%fused_computation | custom fusion | bytes 25182208 | tf_op jit(solution)/shard_map/gather | solution.py:186
  447.8 279.8 %all_to_all.10 = bf16[8,4,128,1536]{3,2,1,0:T(8,128)(2,1)} all-to-all(bf16[8,4,128,1536]{3,2,1,0:T(8,128)(2,1)} %bitcast.179), channel_id=1, replica_groups=mesh['req'=8,'head'=4] {'req'}, dimensions={0} | all-to-all | bytes 25165824 | tf_op jit(solution)/shard_map/all_to_all | solution.py:189
  727.6 23.0 %fusion.53 = f32[8,4,128,1024]{3,2,0,1:T(8,128)} fusion(bf16[4,1536,1024]{2,1,0:T(8,128)(2,1)} %param.26, bf16[8,4,128,1536]{3,2,1,0:T(8,128)(2,1)} %all_to_all.10), kind=kOutput, calls=%fused_computation.62 | convolution fusion | flops 12884901888 | bytes 41943040 | tf_op jit(solution)/shard_map/sncd,ndf->sncf/dot_general | solution.py:187
  750.6 14.8 %fusion.52 = bf16[8,4,128,1536]{3,2,0,1:T(8,128)(2,1)} fusion(bf16[4,512,1536]{2,1,0:T(8,128)(2,1)} %param.27, f32[8,4,128,1024]{3,2,0,1:T(8,128)} %fusion.53), kind=kOutput, calls=%fused_computation.61 | convolution fusion | flops 6461325312 | bytes 35651584 | tf_op jit(solution)/shard_map/sncf,nfd->sncd/dot_general | solution.py:194
  765.4 10.8 copy.52
  781.9 271.8 %all-to-all-done.1 = bf16[8,4,128,1536]{3,2,1,0:T(8,128)(2,1)} async-done(((bf16[8,4,128,1536]{3,2,1,0:T(8,128)(2,1)}), bf16[8,4,128,1536]{3,2,1,0:T(8,128)(2,1)}, u32[]{:S(2)}, u32[]{:S(2)}) %all-to-all-start.1) | async-done | bytes 12582944 | tf_op jit(solution)/shard_map/all_to_all | solution.py:197
  1053.7 19.5 %gather_fusion.1 = bf16[2048,1536]{1,0:T(8,128)(2,1)} fusion(bf16[4096,1536]{1,0:T(8,128)(2,1)} %bitcast.41, s32[2048]{0:T(1024)S(1)} %broadcast_clamp_fusion), kind=kCustom, calls=%fused_computation.1 | custom fusion | bytes 12591104 | tf_op jit(solution)/shard_map/gather | solution.py:198
  1073.2 8.9 fusion.48
  (223 shorter events, 265.8 us)
Async XLA Ops:
  6.5 328.1 %copy-start = (bf16[2,192,1536]{2,1,0:T(8,128)(2,1)S(1)}, bf16[2,192,1536]{2,1,0:T(8,128)(2,1)}, u32[]{:S(2)}) copy-start(bf16[2,192,1536]{2,1,0:T(8,128)(2,1)} %param.22) | copy-start | bytes 3538948
  6.5 36.2 %copy-start.11 = (f32[1536]{0:T(1024)S(1)}, f32[1536]{0:T(1024)}, u32[]{:S(2)}) copy-start(f32[1536]{0:T(1024)} %param.19) | copy-start | bytes 18436
  6.5 33.6 %all-gather.2.cloned.1.call-start = ((), (), s32[]{:S(2)}) async-start(), calls=%async_computation.2 | async-start | bytes 3932160 | tf_op jit(solution)/shard_map/all_gather | solution.py:102
  7.3 417.8 %all-reduce.3.cloned.1.call-start = ((), (), s32[]{:S(2)}) async-start(), calls=%async_computation.3 | async-start | bytes 6291456 | tf_op jit(solution)/shard_map/psum | solution.py:168
  42.7 4.0 copy-start.1
  42.8 4.0 copy-start.10
  48.3 2.4 copy-start.9
  98.4 4.0 copy-start.2
  98.4 4.0 copy-start.3
  205.3 4.0 copy-start.2
  205.3 4.0 copy-start.3
  265.0 4.0 copy-start.2
  265.1 4.0 copy-start.3
  323.6 4.0 copy-start.2
  323.6 4.0 copy-start.3
  334.7 4.7 copy-start.6
  334.7 5.0 copy-start.5
  334.7 14.8 %copy-start.4 = (s32[2048]{0:T(1024)S(1)}, s32[2048]{0:T(1024)}, u32[]{:S(2)}) copy-start(s32[2048]{0:T(1024)} %eq.41) | copy-start | bytes 24580
  334.7 92.1 %copy-start.7 = (f32[1536]{0:T(1024)S(1)}, f32[1536]{0:T(1024)}, u32[]{:S(2)}) copy-start(f32[1536]{0:T(1024)} %param.23) | copy-start | bytes 18436
  776.2 5.6 copy-start.8
  776.2 277.6 %all-to-all-start.1 = ((bf16[8,4,128,1536]{3,2,1,0:T(8,128)(2,1)}), bf16[8,4,128,1536]{3,2,1,0:T(8,128)(2,1)}, u32[]{:S(2)}, u32[]{:S(2)}) async-start(bf16[8,4,128,1536]{3,2,1,0:T(8,128)(2,1)} %copy.52), calls=%async_computation.1 | async-start | bytes 25165824 | tf_op jit(solution)/shard_map/all_to_all | solution.py:197
Sparse Core Ops, SparseCore 0:
  8.9 31.1 all-gather.1
  339.5 85.4 all-reduce.2
where the time goes:
time: 1100 us; the launch traced here: 1090 us
  waiting for transfers between devices  365 us (33%)
  blocking collectives  280 us (25%)
  matrix products  174 us (16%)
  local copies, waits for them, and re-layouts  134 us (12%)
  other arithmetic  108 us (10%)
  between operations  14.2 us (1%)
  loops' own time  11.6 us (1%)
    all_to_all x1, blocking collectives, local(): lax.all_to_all(outgoing, 'req', split_axis=0, concat_axis=0, tiled=True)  280 us
    all_to_all x1, waiting for transfers between devices, local(): lax.all_to_all(produced, 'req', split_axis=0, concat_axis=0, tiled=True)  272 us
    reduce_sum x15, other arithmetic, absorb(): denominator = denominator * rescale + jnp.sum(weights, axis=-1)  71.1 us
    dot_general x15, matrix products, absorb(): jnp.einsum(pattern, weights.astype(jnp.bfloat16), value_rows, preferred_e...  68.7 us
    psum x1, waiting for transfers between devices, local(): lax.psum(partial_value.astype(jnp.bfloat16), 'head').astype(jnp.float32)  67.3 us
    dot_general x11, matrix products, key_step(): jnp.einsum('qhgd,hkd->hgqk', q_win, key_piece[..., :head_size], preferred...  48.9 us
    dynamic_slice x8, local copies, waits for them, and re-layouts, one_request(): past = lax.dynamic_index_in_dim(kv_cache, which, 0, keepdims=False)  42.4 us
    all_gather x1, waiting for transfers between devices, local(): whole = lax.all_gather(tokens, 'head', axis=1, tiled=True)  25 us
  transfers between devices with their start and end apart: 3, of which 3 were waited for; matrix products, arithmetic and copies ran while one was open for 2% of the time, Pallas kernels for 0%

commit v1 on v0

v1 whole, which is shorter than its diff:
```python
import functools
import math

import jax
import jax.numpy as jnp
from jax import lax
from jax.experimental import pallas as pl
from jax.experimental.pallas import tpu as pltpu
from jax.sharding import PartitionSpec as P

EXPERTS = 32
TOPK = 8
RATIO = 15
ROW_TILE = 176
KEY_TILE = 768
PART_TILE = 256
LOW = -1e30
MESH = pl.DeviceIdType.MESH
VMEM_BYTES = 56 * 1024 * 1024


def norm_rows(value_rows, gain_row):
    mean_square = jnp.mean(value_rows * value_rows, axis=-1, keepdims=True)
    return value_rows * lax.rsqrt(mean_square + 1e-05) * gain_row


def rope_tables(position, head_size):
    half_size = head_size // 2
    inverse = jnp.exp(
        jnp.arange(half_size, dtype=jnp.float32) * (-2.0 * math.log(10000.0) / head_size)
    )
    angles = position.astype(jnp.float32)[:, None] * inverse[None, :]
    angles = jnp.concatenate([angles, angles], axis=1)
    return (jnp.cos(angles), jnp.sin(angles))


def rotate(vectors, cos_part, sin_part):
    half_size = vectors.shape[-1] // 2
    turned = jnp.concatenate([-vectors[..., half_size:], vectors[..., :half_size]], axis=-1)
    return vectors * cos_part + turned * sin_part


def request_layout(counts, token_count, cache_ratio):
    end_rows = jnp.cumsum(counts)
    starts = end_rows - counts
    row_ids = jnp.arange(token_count, dtype=jnp.int32)
    segment = jnp.sum((row_ids[:, None] >= end_rows[None, :]).astype(jnp.int32), axis=1)
    member = (segment[:, None] == jnp.arange(counts.shape[0], dtype=jnp.int32)[None, :]).astype(
        jnp.int32
    )
    row_begin = jnp.sum(member * starts[None, :], axis=1)
    own_count = jnp.sum(member * counts[None, :], axis=1)
    position = cache_ratio * own_count + row_ids - row_begin
    return (starts, position)


def greet(axis, length, fast, line_at, fast_at):
    barrier = pltpu.get_barrier_semaphore()

    def to(index):
        pl.semaphore_signal(barrier, inc=1, device_id={axis: index}, device_id_type=MESH)

    for step in range(1, fast):
        to(line_at * fast + lax.rem(fast_at + step, fast))

    @pl.when(line_at > 0)
    def _():
        to((line_at - 1) * fast + fast_at)

    @pl.when(line_at < length - 1)
    def _():
        to((line_at + 1) * fast + fast_at)

    peers = fast - 1
    if length > 1:
        for away in (line_at, length - 1 - line_at):
            peers = peers + lax.div(away + length - 2, length - 1)
    pl.semaphore_wait(barrier, peers)


def gather_kernel(
    axis, length, fast, by_columns, x_ref, out_ref, own_sem, up_s, up_r, down_s, down_r, fast_s, fast_r
):
    me = lax.axis_index(axis)
    line_at, fast_at = me // fast, lax.rem(me, fast)
    width = x_ref.shape[1]

    def place(index):
        if by_columns:
            return out_ref.at[:, pl.ds(pl.multiple_of(index * width, 128), width)]
        return out_ref.at[index]

    greet(axis, length, fast, line_at, fast_at)

    own = pltpu.make_async_copy(x_ref, place(me), own_sem)
    own.start()

    def line_copy(step, sign):
        source = line_at - sign * step
        send, recv = (up_s, up_r) if sign > 0 else (down_s, down_r)
        block = place(source * fast + fast_at)
        return pltpu.make_async_remote_copy(
            src_ref=x_ref if step == 0 else block,
            dst_ref=block,
            send_sem=send.at[step],
            recv_sem=recv.at[step],
            device_id={axis: (line_at + sign) * fast + fast_at},
            device_id_type=MESH,
        )

    def line_arrival(step, sign):
        source = line_at - sign * step
        recv = up_r if sign > 0 else down_r
        block = place(source * fast + fast_at)
        pltpu.make_async_copy(block, block, recv.at[step - 1]).wait()

    def fast_copy(turn, step, sign):
        source = line_at - sign * step
        slot = step if sign > 0 else length - 1 + step
        block = place(source * fast + fast_at)
        return pltpu.make_async_remote_copy(
            src_ref=x_ref if step == 0 else block,
            dst_ref=block,
            send_sem=fast_s.at[turn - 1, slot],
            recv_sem=fast_r.at[turn - 1, slot],
            device_id={axis: line_at * fast + lax.rem(fast_at + turn, fast)},
            device_id_type=MESH,
        )

    def fast_arrival(turn, step, sign):
        source = line_at - sign * step
        slot = step if sign > 0 else length - 1 + step
        block = place(source * fast + lax.rem(fast_at - turn + fast, fast))
        pltpu.make_async_copy(block, block, fast_r.at[turn - 1, slot]).wait()

    def has_next(sign):
        return line_at < length - 1 if sign > 0 else line_at > 0

    def has_source(step, sign):
        return line_at >= step if sign > 0 else line_at + step < length

    for sign in (1, -1):

        @pl.when(has_next(sign))
        def _():
            line_copy(0, sign).start()

    for turn in range(1, fast):
        fast_copy(turn, 0, 1).start()

    for step in range(1, length):
        for sign in (1, -1):

            @pl.when(has_source(step, sign))
            def _():
                line_arrival(step, sign)

                @pl.when(has_next(sign))
                def _():
                    line_copy(step, sign).start()

                for turn in range(1, fast):
                    fast_copy(turn, step, sign).start()

    for turn in range(1, fast):
        fast_arrival(turn, 0, 1)
        fast_copy(turn, 0, 1).wait_send()
    for sign in (1, -1):

        @pl.when(has_next(sign))
        def _():
            line_copy(0, sign).wait_send()

        for step in range(1, length):

            @pl.when(has_source(step, sign))
            def _():
                @pl.when(has_next(sign))
                def _():
                    line_copy(step, sign).wait_send()

                for turn in range(1, fast):
                    fast_arrival(turn, step, sign)
                    fast_copy(turn, step, sign).wait_send()

    own.wait()


def gather_over(value, axis, length, ident, by_columns):
    count = lax.axis_size(axis)
    fast = count // length
    rows, width = value.shape
    shape = (rows, count * width) if by_columns else (count, rows, width)
    dma = pltpu.SemaphoreType.DMA
    return pl.pallas_call(
        functools.partial(gather_kernel, axis, length, fast, by_columns),
        out_shape=jax.ShapeDtypeStruct(shape, value.dtype),
        in_specs=[pl.BlockSpec(memory_space=pl.ANY)],
        out_specs=pl.BlockSpec(memory_space=pl.ANY),
        scratch_shapes=[
            dma,
            dma((length,)),
            dma((length,)),
            dma((length,)),
            dma((length,)),
            dma((max(fast - 1, 1), 2 * length - 1)),
            dma((max(fast - 1, 1), 2 * length - 1)),
        ],
        compiler_params=pltpu.CompilerParams(
            collective_id=ident, has_side_effects=True, vmem_limit_bytes=VMEM_BYTES
        ),
        name="gather_" + axis,
    )(value)


def scatter_kernel(
    axis, length, fast, parts_ref, out_ref, near, up_in, down_in, up_out, down_out,
    near_s, near_r, up_s, up_r, down_s, down_r,
):
    me = lax.axis_index(axis)
    line_at, fast_at = me // fast, lax.rem(me, fast)
    rows = out_ref.shape[0]
    chunk = 32
    greet(axis, length, fast, line_at, fast_at)

    def slot_of(step, sign):
        return step if sign > 0 else length - 1 + step

    def there(step, sign):
        return line_at + step < length if sign > 0 else line_at >= step

    def near_copy(turn, step, sign):
        target = line_at + sign * step
        other = lax.rem(fast_at + turn, fast)
        return pltpu.make_async_remote_copy(
            src_ref=parts_ref.at[target * fast + other],
            dst_ref=near.at[turn - 1, target],
            send_sem=near_s.at[turn - 1, slot_of(step, sign)],
            recv_sem=near_r.at[turn - 1, slot_of(step, sign)],
            device_id={axis: line_at * fast + other},
            device_id_type=MESH,
        )

    def line_copy(step, sign):
        outgoing, incoming = (up_out, up_in) if sign > 0 else (down_out, down_in)
        send, recv = (up_s, up_r) if sign > 0 else (down_s, down_r)
        return pltpu.make_async_remote_copy(
            src_ref=outgoing.at[step - 1],
            dst_ref=incoming.at[step - 1],
            send_sem=send.at[step - 1],
            recv_sem=recv.at[step - 1],
            device_id={axis: (line_at + sign) * fast + fast_at},
            device_id_type=MESH,
        )

    def start_near(step):
        for sign in (1, -1) if step > 0 else (1,):

            @pl.when(there(step, sign))
            def _():
                for turn in range(1, fast):
                    near_copy(turn, step, sign).start()

    def add_up(target, extra, store):
        @pl.loop(0, rows // chunk)
        def _(piece):
            span = pl.ds(pl.multiple_of(piece * chunk, chunk), chunk)
            total = parts_ref[target * fast + fast_at, span, :].astype(jnp.float32)
            for turn in range(1, fast):
                total = total + near[turn - 1, target, span, :].astype(jnp.float32)
            for incoming, slot in extra:
                total = total + incoming[slot, span, :].astype(jnp.float32)
            store(span, total)

    def near_arrival(step, sign):
        for turn in range(1, fast):
            near_copy(turn, step, sign).wait_recv()

    start_near(length - 1)
    if length > 1:
        start_near(length - 2)
    for step in range(length - 1, 0, -1):
        for sign in (1, -1):
            outgoing, incoming = (up_out, up_in) if sign > 0 else (down_out, down_in)
            has_before = line_at > 0 if sign > 0 else line_at < length - 1

            def store(span, total):
                outgoing[step - 1, span, :] = total.astype(outgoing.dtype)

            @pl.when(there(step, sign))
            def _():
                near_arrival(step, sign)
                target = line_at + sign * step
                if step < length - 1:

                    @pl.when(has_before)
                    def _():
                        line_copy(step + 1, sign).wait_recv()
                        add_up(target, [(incoming, step)], store)

                    @pl.when(jnp.logical_not(has_before))
                    def _():
                        add_up(target, [], store)
                else:
                    add_up(target, [], store)
                line_copy(step, sign).start()

        if step >= 2:
            start_near(step - 2)

    near_arrival(0, 1)

    def store_out(span, total):
        out_ref[span, :] = total

    def add_out(span, total):
        out_ref[span, :] = out_ref[span, :] + total

    add_up(line_at, [], store_out)
    if length > 1:
        for sign in (1, -1):
            incoming = up_in if sign > 0 else down_in
            has_before = line_at > 0 if sign > 0 else line_at < length - 1

            @pl.when(has_before)
            def _():
                line_copy(1, sign).wait_recv()

                @pl.loop(0, rows // chunk)
                def _(piece):
                    span = pl.ds(pl.multiple_of(piece * chunk, chunk), chunk)
                    add_out(span, incoming[0, span, :].astype(jnp.float32))

    for step in range(length - 1, -1, -1):
        for sign in (1, -1) if step > 0 else (1,):

            @pl.when(there(step, sign))
            def _():
                for turn in range(1, fast):
                    near_copy(turn, step, sign).wait_send()
                if step > 0:
                    line_copy(step, sign).wait_send()


def scatter_over(parts, axis, length, ident):
    count, rows, width = parts.shape
    fast = count // length
    dma = pltpu.SemaphoreType.DMA
    hops = max(length - 1, 1)
    turns = max(fast - 1, 1)
    line_shape = pltpu.VMEM((hops, rows, width), parts.dtype)
    return pl.pallas_call(
        functools.partial(scatter_kernel, axis, length, fast),
        out_shape=jax.ShapeDtypeStruct((rows, width), jnp.float32),
        in_specs=[pl.BlockSpec(memory_space=pltpu.VMEM)],
        out_specs=pl.BlockSpec(memory_space=pltpu.VMEM),
        scratch_shapes=[
            pltpu.VMEM((turns, length, rows, width), parts.dtype),
            line_shape,
            line_shape,
            line_shape,
            line_shape,
            dma((turns, 2 * length - 1)),
            dma((turns, 2 * length - 1)),
            dma((hops,)),
            dma((hops,)),
            dma((hops,)),
            dma((hops,)),
        ],
        compiler_params=pltpu.CompilerParams(
            collective_id=ident, has_side_effects=True, vmem_limit_bytes=VMEM_BYTES
        ),
        name="scatter_" + axis,
    )(parts)


def attend_kernel(starts_ref, counts_ref, q_ref, key_ref, value_ref, past_ref, out_ref, top_ref, sum_ref):
    which = pl.program_id(1)
    begin = starts_ref[which]
    count = counts_ref[which]
    cached = RATIO * count
    base = (begin // 16) * 16
    heads = q_ref.shape[1]
    size = out_ref.shape[3]
    tiles = (begin + count - base + ROW_TILE - 1) // ROW_TILE
    whole = cached // KEY_TILE
    rest = (cached - whole * KEY_TILE + PART_TILE - 1) // PART_TILE

    def absorb(head, query, keys, values, ok):
        scores = lax.dot_general(
            query, keys, (((1,), (1,)), ((), ())), preferred_element_type=jnp.float32
        )
        if ok is not None:
            scores = jnp.where(ok, scores, LOW)
        old_top = top_ref[head]
        new_top = jnp.maximum(old_top, jnp.max(scores, axis=1, keepdims=True))
        top_ref[head] = new_top
        weights = jnp.exp2((scores - new_top[:, :1]).astype(jnp.bfloat16))
        sum_ref[head] = sum_ref[head] * jnp.exp2(old_top - new_top) + jnp.dot(
            weights, values, preferred_element_type=jnp.float32
        )

    @pl.loop(0, tiles)
    def _(tile):
        row = pl.multiple_of(base + tile * ROW_TILE, 16)
        span = pl.ds(row, ROW_TILE)
        for head in range(heads):
            top_ref[head] = jnp.full(top_ref.shape[1:], LOW, jnp.float32)
            sum_ref[head] = jnp.zeros(sum_ref.shape[1:], jnp.float32)

        new_blocks = (row + ROW_TILE - base + PART_TILE - 1) // PART_TILE

        @pl.loop(0, new_blocks)
        def _(block):
            first = pl.multiple_of(base + block * PART_TILE, 16)
            keys = key_ref[0, pl.ds(first, PART_TILE), :]
            values = value_ref[0, pl.ds(first, PART_TILE), :]
            key_rows = first + lax.broadcasted_iota(jnp.int32, (ROW_TILE, PART_TILE), 1)
            own_rows = row + lax.broadcasted_iota(jnp.int32, (ROW_TILE, PART_TILE), 0)
            ok = (key_rows >= begin) & (key_rows <= own_rows)
            for head in range(heads):
                absorb(head, q_ref[0, head, span, :], keys, values, ok)

        def cache_rows(first, amount):
            keys = past_ref[0, 0, pl.ds(first, amount), :]
            lanes = lax.broadcasted_iota(jnp.int32, keys.shape, 1)
            return keys, jnp.where(lanes < size, jnp.ones_like(keys), keys)

        @pl.loop(0, whole)
        def _(block):
            keys, values = cache_rows(pl.multiple_of(block * KEY_TILE, KEY_TILE), KEY_TILE)
            for head in range(heads):
                absorb(head, q_ref[0, head, span, :], keys, values, None)

        @pl.loop(0, rest)
        def _(block):
            first = pl.multiple_of(whole * KEY_TILE + block * PART_TILE, PART_TILE)
            keys, values = cache_rows(first, PART_TILE)
            slots = first + lax.broadcasted_iota(jnp.int32, (ROW_TILE, PART_TILE), 1)
            for head in range(heads):
                absorb(head, q_ref[0, head, span, :], keys, values, slots < cached)

        rows = row + lax.broadcasted_iota(jnp.int32, (ROW_TILE, size), 0)
        inside = (rows >= begin) & (rows < begin + count)
        for head in range(heads):
            total = sum_ref[head]
            attended = (total[:, size:] / total[:, :size]).astype(out_ref.dtype)
            out_ref[0, head, span, :] = jnp.where(inside, attended, out_ref[0, head, span, :])


def attend(starts, counts, query, keys, values, kv_cache):
    kv_heads, heads, rows, lanes = query.shape
    requests, _, slots, _ = kv_cache.shape
    size = lanes // 2
    return pl.pallas_call(
        attend_kernel,
        out_shape=jax.ShapeDtypeStruct((kv_heads, heads, rows, size), jnp.bfloat16),
        grid_spec=pltpu.PrefetchScalarGridSpec(
            num_scalar_prefetch=2,
            grid=(kv_heads, requests),
            in_specs=[
                pl.BlockSpec((1, heads, rows, lanes), lambda h, r, s, c: (h, 0, 0, 0)),
                pl.BlockSpec((1, rows, lanes), lambda h, r, s, c: (h, 0, 0)),
                pl.BlockSpec((1, rows, lanes), lambda h, r, s, c: (h, 0, 0)),
                pl.BlockSpec((1, 1, slots, lanes), lambda h, r, s, c: (r, h, 0, 0)),
            ],
            out_specs=pl.BlockSpec((1, heads, rows, size), lambda h, r, s, c: (h, 0, 0, 0)),
            scratch_shapes=[
                pltpu.VMEM((heads, ROW_TILE, lanes), jnp.float32),
                pltpu.VMEM((heads, ROW_TILE, lanes), jnp.float32),
            ],
        ),
        compiler_params=pltpu.CompilerParams(vmem_limit_bytes=VMEM_BYTES),
        name="attend",
    )(starts, counts, query, keys, values, kv_cache)


def expert_kernel(
    capacity, rank_row_ref, rank_col_ref, gain_col_ref, x_ref, up_hbm, down_hbm, out_ref,
    up_ref, down_ref, total_ref, sems,
):
    group, per_block, _ = x_ref.shape
    experts = up_ref.shape[0]
    ff_width = down_ref.shape[1]
    first = pl.program_id(0) == 0

    def fetch(expert):
        return (
            pltpu.make_async_copy(up_hbm.at[expert], up_ref.at[expert], sems.at[0, expert]),
            pltpu.make_async_copy(down_hbm.at[expert], down_ref.at[expert], sems.at[1, expert]),
        )

    @pl.when(first)
    def _():
        for expert in range(experts):
            for copy in fetch(expert):
                copy.start()

    for expert in range(experts):

        @pl.when(first)
        def _():
            for copy in fetch(expert):
                copy.wait()

        slot_rows = lax.broadcasted_iota(jnp.int32, (capacity, per_block), 0)
        slot_cols = lax.broadcasted_iota(jnp.int32, (per_block, capacity), 1)
        picked = []
        for item in range(group):
            ranks = rank_row_ref[item, expert : expert + 1, :]
            choose = (slot_rows == ranks).astype(jnp.float32).astype(jnp.bfloat16)
            picked.append(
                jnp.dot(choose, x_ref[item], preferred_element_type=jnp.float32).astype(jnp.bfloat16)
            )
        picked = jnp.concatenate(picked, axis=0)
        both = jnp.dot(picked, up_ref[expert], preferred_element_type=jnp.float32)
        gate = both[:, :ff_width]
        hidden = (gate / (1.0 + jnp.exp(-gate)) * both[:, ff_width:]).astype(jnp.bfloat16)
        made = jnp.dot(hidden, down_ref[expert], preferred_element_type=jnp.float32).astype(
            jnp.bfloat16
        )
        for item in range(group):
            ranks = rank_col_ref[item, :, expert : expert + 1]
            gains = gain_col_ref[item, :, expert : expert + 1]
            blend = jnp.where(slot_cols == ranks, gains, 0.0).astype(jnp.bfloat16)
            part = jnp.dot(
                blend,
                made[item * capacity : (item + 1) * capacity],
                preferred_element_type=jnp.float32,
            )
            if expert > 0:
                part = total_ref[item] + part
            if expert < experts - 1:
                total_ref[item] = part
            else:
                out_ref[item] = part.astype(out_ref.dtype)


def run_experts(rank_col, gain_col, rows, w_gate_up, w_down, capacity):
    sources, per_block, width = rows.shape
    experts = w_down.shape[0]
    group = min(sources, max(1, 256 // capacity))
    rank_row = jnp.swapaxes(rank_col, 1, 2)
    return pl.pallas_call(
        functools.partial(expert_kernel, capacity),
        out_shape=jax.ShapeDtypeStruct((sources, per_block, width), jnp.bfloat16),
        grid=(sources // group,),
        in_specs=[
            pl.BlockSpec((group, experts, per_block), lambda s: (s, 0, 0)),
            pl.BlockSpec((group, per_block, experts), lambda s: (s, 0, 0)),
            pl.BlockSpec((group, per_block, experts), lambda s: (s, 0, 0)),
            pl.BlockSpec((group, per_block, width), lambda s: (s, 0, 0)),
            pl.BlockSpec(memory_space=pl.ANY),
            pl.BlockSpec(memory_space=pl.ANY),
        ],
        out_specs=pl.BlockSpec((group, per_block, width), lambda s: (s, 0, 0)),
        scratch_shapes=[
            pltpu.VMEM(w_gate_up.shape, w_gate_up.dtype),
            pltpu.VMEM(w_down.shape, w_down.dtype),
            pltpu.VMEM((group, per_block, width), jnp.float32),
            pltpu.SemaphoreType.DMA((2, experts)),
        ],
        compiler_params=pltpu.CompilerParams(vmem_limit_bytes=VMEM_BYTES),
        name="experts",
    )(rank_row, rank_col, gain_col, rows, w_gate_up, w_down)


def local(
    req_line,
    head_line,
    tokens,
    new_counts,
    kv_cache,
    norm_attn,
    query_weight,
    key_value_weight,
    output_weight,
    norm_moe,
    routes,
    route_gain,
    w_gate_up,
    w_down,
):
    per_block = routes.shape[0]
    capacity = per_block // 2
    per_req = w_down.shape[0]

    table = jnp.concatenate([routes.astype(jnp.float32), route_gain], axis=1)
    table = lax.all_gather(table, "req", axis=0)
    all_routes = table[..., :TOPK]
    own_ids = lax.axis_index("req") * per_req + jnp.arange(per_req, dtype=jnp.int32)
    named = all_routes[:, :, :, None] == own_ids.astype(jnp.float32)[None, None, None, :]
    chosen = jnp.any(named, axis=2)
    gain_col = jnp.sum(jnp.where(named, table[..., TOPK:, None], 0.0), axis=2)
    earlier = jnp.tril(jnp.ones((per_block, per_block), jnp.bfloat16), -1)
    rank_col = jnp.einsum(
        "tu,sun->stn", earlier, chosen.astype(jnp.bfloat16), preferred_element_type=jnp.float32
    )
    rank_col = jnp.where(chosen, rank_col.astype(jnp.int32), -1)

    if tokens.shape[1] % 128 == 0:
        whole = gather_over(tokens, "head", head_line, 0, True)
    else:
        narrow = tokens.shape[1]
        spread = jnp.pad(tokens, ((0, 0), (0, -narrow % 128)))
        whole = gather_over(spread, "head", head_line, 0, False)[..., :narrow]
        whole = jnp.swapaxes(whole, 0, 1).reshape(tokens.shape[0], -1)
    token_count, model_width = whole.shape
    normed = norm_rows(whole.astype(jnp.float32), norm_attn).astype(jnp.bfloat16)
    counts = new_counts[0]
    starts, position = request_layout(counts, token_count, RATIO)
    kv_heads = key_value_weight.shape[1]
    size = key_value_weight.shape[2] // 2
    groups = query_weight.shape[2] // size
    cos_part, sin_part = rope_tables(position, size)
    query = jnp.dot(
        normed, query_weight.reshape(model_width, -1), preferred_element_type=jnp.float32
    ).reshape(token_count, kv_heads, groups, size)
    keyval = jnp.dot(
        normed, key_value_weight.reshape(model_width, -1), preferred_element_type=jnp.float32
    ).reshape(token_count, kv_heads, 2 * size)
    scale = math.log2(math.e) / math.sqrt(size)
    query = rotate(query, cos_part[:, None, None, :], sin_part[:, None, None, :]) * scale
    query = jnp.transpose(query.astype(jnp.bfloat16), (1, 2, 0, 3))
    new_key = rotate(keyval[..., :size], cos_part[:, None, :], sin_part[:, None, :])
    new_key = jnp.transpose(new_key.astype(jnp.bfloat16), (1, 0, 2))
    new_value = jnp.transpose(keyval[..., size:].astype(jnp.bfloat16), (1, 0, 2))
    spare = 512
    query = jnp.pad(query, ((0, 0), (0, 0), (0, spare), (0, size)))
    new_key = jnp.pad(new_key, ((0, 0), (0, spare), (0, size)))
    new_value = jnp.pad(
        jnp.concatenate([jnp.ones_like(new_value), new_value], axis=2), ((0, 0), (0, spare), (0, 0))
    )
    attended = attend(starts, counts, query, new_key, new_value, kv_cache)[:, :, :token_count]
    flat = jnp.transpose(attended, (2, 0, 1, 3)).reshape(token_count, -1)
    partial_value = jnp.dot(
        flat, output_weight.reshape(-1, model_width), preferred_element_type=jnp.float32
    ).astype(jnp.bfloat16)
    attn_rows = scatter_over(
        partial_value.reshape(-1, per_block, model_width), "head", head_line, 1
    )
    row_start = lax.axis_index("head") * per_block
    base_rows = lax.dynamic_slice_in_dim(whole, row_start, per_block, 0)
    resid = base_rows.astype(jnp.float32) + attn_rows
    moe_in = norm_rows(resid, norm_moe).astype(jnp.bfloat16)
    everyone = gather_over(moe_in, "req", req_line, 2, False)
    parts = run_experts(rank_col, gain_col, everyone, w_gate_up, w_down, capacity)
    moe_sum = scatter_over(parts, "req", req_line, 3)
    return (resid + moe_sum).astype(jnp.bfloat16)


def solution(mesh):
    in_specs = (
        P("req", "head"),
        P("req", None),
        P("req", "head", None, None),
        P(),
        P(None, "head", None),
        P(None, "head", None),
        P("head", None, None),
        P(),
        P(("req", "head"), None),
        P(("req", "head"), None),
        P("req", None, None),
        P("req", None, None),
    )
    out_specs = P(("req", "head"), None)
    head_line = max(mesh.shape["head"] // 2, 1)
    req_line = math.gcd(mesh.shape["req"], 4)
    body = functools.partial(local, req_line, head_line)
    return jax.shard_map(body, mesh=mesh, in_specs=in_specs, out_specs=out_specs, check_vma=False)
```

time: 1100 us -> 530 us (0.48)
  Pallas kernels: 0 us -> 454 us
  waiting for transfers between devices: 365 us -> 0 us
  blocking collectives: 280 us -> 32.3 us
  matrix products: 174 us -> 8.62 us
  local copies, waits for them, and re-layouts: 134 us -> 13.1 us
  other arithmetic: 108 us -> 21.1 us
  between operations: 14.2 us -> 0.23 us
  loops' own time: 11.6 us -> 0 us
    pallas_call x0 -> x6, Pallas kernels: none -> 454 us  [the longest x1 192 us: attend(): pl.pallas_call(attend_kernel, out_shape=jax.ShapeDtypeStruct((kv_heads, h...]
    all_to_all x1 -> x0, blocking collectives: 280 us -> none  [local(): lax.all_to_all(outgoing, 'req', split_axis=0, concat_axis=0, tiled=True)]
    all_to_all x1 -> x0, waiting for transfers between devices: 272 us -> none  [local(): lax.all_to_all(produced, 'req', split_axis=0, concat_axis=0, tiled=True)]
    dot_general x35 -> x4, matrix products: 174 us -> 8.62 us  [the longest x1 3.54 us: local(): jnp.dot(flat, output_weight.reshape(-1, model_width), preferred_element_t...]
    reduce_sum x17 -> x1, other arithmetic: 80.1 us -> 0.16 us  [local(): gain_col = jnp.sum(jnp.where(named, table[..., TOPK:, None], 0.0), axis=2)]
    psum x1 -> x0, waiting for transfers between devices: 67.3 us -> none  [local(): lax.psum(partial_value.astype(jnp.bfloat16), 'head').astype(jnp.float32)]
    dynamic_slice x24 -> x0, local copies, waits for them, and re-layouts: 48.7 us -> none  [the longest x8 42.4 us: one_request(): past = lax.dynamic_index_in_dim(kv_cache, which, 0, keepdims=False)]
    gather x2 -> x0, local copies, waits for them, and re-layouts: 38.7 us -> none  [the longest x1 19.5 us: local(): arrived.reshape(EXPERTS * capacity, model_width)[slot_ids]]
  transfers between devices with their start and end apart: 3 -> 0, of which waited for: 3 -> 0; matrix products, arithmetic and copies ran while one was open for 2% -> 0% of each run, Pallas kernels for 0% -> 0%
where the time goes in v1:
time: 530 us; the launch traced here: 529 us
  Pallas kernels  454 us (86%)
  blocking collectives  32.3 us (6%)
  other arithmetic  21.1 us (4%)
  local copies, waits for them, and re-layouts  13.1 us (2%)
  matrix products  8.62 us (2%)
    pallas_call x1, Pallas kernels, attend(): pl.pallas_call(attend_kernel, out_shape=jax.ShapeDtypeStruct((kv_heads, h...  192 us
    pallas_call x2, Pallas kernels, gather_over(): pl.pallas_call(functools.partial(gather_kernel, axis, length, fast, by_co...  126 us
    pallas_call x2, Pallas kernels, scatter_over(): pl.pallas_call(functools.partial(scatter_kernel, axis, length, fast), out...  96.9 us
    pallas_call x1, Pallas kernels, run_experts(): pl.pallas_call(functools.partial(expert_kernel, capacity), out_shape=jax....  39.1 us
    all_gather x1, blocking collectives, local(): table = lax.all_gather(table, 'req', axis=0)  32.3 us

profile of v1, /device:TPU:0, one launch (start us, length us, event | category | flops | bytes accessed | tf_op | source)
XLA Modules:
  0.0 529.2 jit_solution(4942780656439824549)
XLA Ops:
  0.0 1.3 copy-done
  2.1 1.2 bitcast_subtract_fusion.1.starts_ref
  6.2 32.3 %all-gather = f32[2048,16]{0,1:T(8,128)S(1)} all-gather(f32[256,16]{0,1:T(8,128)S(1)} %pad_maximum_fusion.1), channel_id=2, replica_groups=mesh['req'=8,'head'=4] {'req'}, dimensions={0}, use_global_device_ids=true | all-gather | bytes 147456 | tf_op jit(solution)/shard_map/all_gather | solution.py:589
  39.6 2.2 fusion.19
  41.9 1.2 copy.65
  43.1 1.2 copy.43
  44.3 1.4 copy.55.gain_col_ref
  45.7 1.4 bitcast_select_fusion.1
  47.1 2.2 copy.54.rank_row_ref
  50.3 26.6 %gather_head.1 = bf16[1024,1536]{1,0:T(8,128)(2,1)} custom-call(bf16[1024,384]{1,0:T(8,128)(2,1)} %x_ref.1), custom_call_target="tpu_custom_call" | custom-call | tf_op jit(solution)/shard_map/gather_head/pallas_call | solution.py:195
  76.9 2.7 fusion
  81.0 1.2 fusion.11.value_ref
  83.9 2.7 fusion.6
  88.7 1.8 pad.13.q_ref
  90.5 192.3 %attend.1 = bf16[2,3,1536,64]{3,2,1,0:T(8,128)(2,1)} custom-call(s32[4]{0:T(128)} %bitcast_subtract_fusion.1.starts_ref, s32[4]{0:T(128)} %bitcast.71, bf16[2,3,1536,128]{3,2,1,0:T(8,128)(2,1)} %pad.13.q_ref, bf16[2,1536,128]{2,1,0:T(8,128)(2,1)} %pad.14.key_ref, bf16[2,1536,128]{2,1,0:T(8,128)(2,1)} %fusion.11.value_ref, bf16[4,2,7680,128]{3,2,1,0:T(8,128)(2,1)} %past_ref.1), custom_call_target="tpu_custom_call" | custom-call | tf_op jit(solution)/shard_map/attend/pallas_call | solution.py:455
  282.8 1.5 slice_bitcast_fusion
  285.0 3.5 convolution_convert_fusion
  288.6 24.0 %scatter_head.1 = f32[256,1536]{1,0:T(8,128)} custom-call(bf16[4,256,1536]{2,1,0:T(8,128)(2,1)} %bitcast.62), custom_call_target="tpu_custom_call" | custom-call | tf_op jit(solution)/shard_map/scatter_head/pallas_call | solution.py:352
  312.7 1.8 multiply_reduce_fusion
  314.5 1.1 multiply_convert_fusion.x_ref
  315.7 99.0 %gather_req.1.x_ref = bf16[8,256,1536]{2,1,0:T(8,128)(2,1)} custom-call(bf16[256,1536]{1,0:T(8,128)(2,1)} %multiply_convert_fusion.x_ref), custom_call_target="tpu_custom_call" | custom-call | tf_op jit(solution)/shard_map/gather_req/pallas_call | solution.py:195
  414.6 39.1 %experts.1.parts_ref = bf16[8,256,1536]{2,1,0:T(8,128)(2,1)} custom-call(s32[8,4,256]{2,1,0:T(4,128)} %copy.54.rank_row_ref, s32[8,256,4]{2,1,0:T(8,128)} %bitcast_select_fusion.rank_col_ref, f32[8,256,4]{2,1,0:T(8,128)} %copy.55.gain_col_ref, bf16[8,256,1536]{2,1,0:T(8,128)(2,1)} %gather_req.1.x_ref, bf16[4,1536,1024]{2,1,0:T(8,128)(2,1)} %up_hbm.1, ...), custom_call_target="tpu_custom_call" | custom-call | tf_op jit(solution)/shard_map/experts/pallas_call | solution.py:544
  453.7 72.8 %scatter_req.1 = f32[256,1536]{1,0:T(8,128)} custom-call(bf16[8,256,1536]{2,1,0:T(8,128)(2,1)} %experts.1.parts_ref), custom_call_target="tpu_custom_call" | custom-call | tf_op jit(solution)/shard_map/scatter_req/pallas_call | solution.py:352
  526.6 2.7 add_convert_fusion
  (44 shorter events, 11.9 us)
Async XLA Ops:
  0.0 1.3 copy-start
  50.3 29.3 %copy-start.4 = (bf16[256,1536]{1,0:T(8,128)(2,1)S(1)}, bf16[256,1536]{1,0:T(8,128)(2,1)}, u32[]{:S(2)}) copy-start(bf16[256,1536]{1,0:T(8,128)(2,1)} %copy.43) | copy-start | bytes 2359300
  50.3 29.3 %copy-start.7 = (f32[1536]{0:T(1024)S(1)}, f32[1536]{0:T(1024)}, u32[]{:S(2)}) copy-start(f32[1536]{0:T(1024)} %param.15) | copy-start | bytes 18436
  76.9 2.8 copy-start.2
  82.5 1.5 copy-start.6
  288.6 24.1 %copy-start.3 = (bf16[1024,1536]{1,0:T(8,128)(2,1)S(1)}, bf16[1024,1536]{1,0:T(8,128)(2,1)}, u32[]{:S(2)}) copy-start(bf16[1024,1536]{1,0:T(8,128)(2,1)} %gather_head.1) | copy-start | bytes 9437188
  288.6 25.9 %copy-start.5 = (f32[1536]{0:T(1024)S(1)}, f32[1536]{0:T(1024)}, u32[]{:S(2)}) copy-start(f32[1536]{0:T(1024)} %param.19) | copy-start | bytes 18436
  312.6 1.9 copy-start.1
